TPU v7x, 256 devices: a whole 4x4x8 slice. The times are simulated.
256 devices in a mesh: dp: 8 (over z), group: 4 (over x), tensor: 8 (over y, core).
Axes of the slice: x: 4, y: 4, z: 8, core: 2. Of those that a mesh axis runs over, the one named last changes fastest.
Arguments:
- learn_x: bfloat16 [32768, 8192], P(('dp', 'group'), 'tensor'), may hold values from -6.5 to 6.5
- learn_dy: bfloat16 [32768, 1024], P(('dp', 'group'), 'tensor'), may hold values from -0.59765625 to 0.59765625
- block_tenant: int32 [256], P(('dp', 'group')), may hold values from 0 to 63, as said below
- block_count: int32 [256], P(('dp', 'group')), may hold values from 32 to 128
- adapter_a: float32 [64, 32, 8192], P(('dp', 'group'), None, 'tensor'), may hold values from -0.0625 to 0.0625
- adapter_b: float32 [64, 32, 1024], P(('dp', 'group'), None, 'tensor'), may hold values from -0.1875 to 0.1875
- moment_a: float32 [64, 32, 8192], P(('dp', 'group'), None, 'tensor'), may hold values from -12 to 12
- moment_b: float32 [64, 32, 1024], P(('dp', 'group'), None, 'tensor'), may hold values from -12 to 12
- second_a: float32 [64, 32, 8192], P(('dp', 'group'), None, 'tensor'), may hold values from 0.01 to 0.5
- second_b: float32 [64, 32, 1024], P(('dp', 'group'), None, 'tensor'), may hold values from 0.01 to 0.5
- tenant_group: int32 [64], replicated, may hold values from 0 to 3, as said below
- decode_inputs: bfloat16 [4, 1024, 2, 8192], P('group', 'dp'), may hold values from -6.5 to 6.5
- dec_weight: bfloat16 [8192, 1024], P(None, 'tensor'), may hold values from -0.0625 to 0.0625
- request_adapter: int32 [4, 1024], P('group', 'dp'), may hold values from 0 to 63, as said below
Outputs:
- updated_a: float32 [64, 32, 8192], P(('dp', 'group'), None, 'tensor')
- updated_b: float32 [64, 32, 1024], P(('dp', 'group'), None, 'tensor')
- moment_a_new: float32 [64, 32, 8192], P(('dp', 'group'), None, 'tensor')
- moment_b_new: float32 [64, 32, 1024], P(('dp', 'group'), None, 'tensor')
- second_a_new: float32 [64, 32, 8192], P(('dp', 'group'), None, 'tensor')
- second_b_new: float32 [64, 32, 1024], P(('dp', 'group'), None, 'tensor')
- decode_output: bfloat16 [4, 1024, 2, 1024], P('group', 'dp', None, 'tensor')
Inputs may be any that keep to these rules, and one draw needn't show every extreme that they name: `block_tenant`: the state of tenant t lies on index t // 2 of dp+group, whose group index is (t // 2) % 4. The 8 blocks of one device (one index of dp+group) name tenants of each group index exactly 8 / 4 times, in any order. `tenant_group`: for each index i of dp, the tenants i * 8 to (i + 1) * 8 - 1 include exactly 2 tenants of each group; so each group serves exactly 16 tenants. Each request's tenant is served by the request's group: tenant_group[request_adapter[g, q]] == g; every tenant that a group serves is named by some request of that group.
All inputs are finite; a program needn't handle non-finite values.
Results may differ from a plain program's by a relative error of at most 0.012.
Values may be sent and summed in bfloat16 or wider, within the bound.
No kernel may reach another device: no remote copies, remote signals or barrier semaphores. Data moves between devices by JAX's collectives and lax.ppermute only.
A program may use at most 64 MiB of HBM per device.

v0:
```python
import jax
import jax.numpy as jnp
from jax import lax
from jax.sharding import PartitionSpec as P

STEP_NUM = 10


adapter_scale = 2.0
beta_one = 0.9
beta_two = 0.999
step_rate = 0.001
adam_eps = 1e-08


def adam_update(weights, moment, second, gradient):
    moment_new = beta_one * moment + (1.0 - beta_one) * gradient
    second_new = beta_two * second + (1.0 - beta_two) * gradient * gradient
    unbiased_m = moment_new / (1.0 - beta_one**STEP_NUM)
    unbiased_v = second_new / (1.0 - beta_two**STEP_NUM)
    weights_new = weights - step_rate * unbiased_m / (jnp.sqrt(unbiased_v) + adam_eps)
    return (weights_new, moment_new, second_new)


def local(
    learn_x,
    learn_dy,
    block_tenant,
    block_count,
    adapter_a,
    adapter_b,
    moment_a,
    moment_b,
    second_a,
    second_b,
    tenant_group,
    decode_inputs,
    dec_weight,
    request_adapter,
):
    block_total = block_tenant.shape[0]
    width_a = learn_x.shape[1]
    width_b = learn_dy.shape[1]
    block_rows = learn_x.shape[0] // block_total
    owned = adapter_a.shape[0]
    input_blocks = learn_x.reshape(block_total, block_rows, width_a)
    alive_rows = (jnp.arange(block_rows, dtype=jnp.int32)[None, :] < block_count[:, None]).astype(
        jnp.bfloat16
    )
    cotan_blocks = learn_dy.reshape(block_total, block_rows, width_b) * alive_rows[:, :, None]
    a_half = adapter_a.astype(jnp.bfloat16)
    b_half = adapter_b.astype(jnp.bfloat16)
    piece_a = lax.all_gather(a_half, ("dp", "group"), axis=0, tiled=True)
    piece_b = lax.all_gather(b_half, ("dp", "group"), axis=0, tiled=True)
    row_count = piece_a.shape[0]
    chosen = (block_tenant[:, None] == jnp.arange(row_count, dtype=jnp.int32)[None, :]).astype(
        jnp.bfloat16
    )
    add_a = jnp.einsum("bt,trd->brd", chosen, piece_a, preferred_element_type=jnp.float32)
    add_b = jnp.einsum("bt,trk->brk", chosen, piece_b, preferred_element_type=jnp.float32)
    sel_a = add_a
    sel_b = add_b
    sel_a = sel_a.astype(jnp.bfloat16)
    sel_b = sel_b.astype(jnp.bfloat16)
    in_part = jnp.einsum("bnd,brd->bnr", input_blocks, sel_a, preferred_element_type=jnp.float32)
    back_part = jnp.einsum("bnk,brk->bnr", cotan_blocks, sel_b, preferred_element_type=jnp.float32)
    in_total, back_total = (
        lax.psum(in_part.astype(jnp.bfloat16), "tensor").astype(jnp.float32),
        lax.psum(back_part.astype(jnp.bfloat16), "tensor").astype(jnp.float32),
    )
    low_rank_input = in_total.astype(jnp.bfloat16)
    low_rank_backward = back_total.astype(jnp.bfloat16)
    down_gradient_blocks = adapter_scale * jnp.einsum(
        "bnr,bnd->brd", low_rank_backward, input_blocks, preferred_element_type=jnp.float32
    )
    up_gradient_blocks = adapter_scale * jnp.einsum(
        "bnr,bnk->brk", low_rank_input, cotan_blocks, preferred_element_type=jnp.float32
    )
    grad_blocks = jnp.concatenate([down_gradient_blocks, up_gradient_blocks], axis=2)
    chosen = (
        jnp.arange(lax.axis_size(("dp", "group")) * owned, dtype=jnp.int32)[:, None]
        == block_tenant[None, :]
    ).astype(jnp.float32)
    gradients = lax.psum_scatter(
        jnp.einsum("tb,brw->trw", chosen, grad_blocks, precision=lax.Precision.HIGHEST).astype(
            jnp.bfloat16
        ),
        ("dp", "group"),
        scatter_dimension=0,
        tiled=True,
    ).astype(jnp.float32)
    updated_a, moment_a_new, second_a_new = adam_update(
        adapter_a, moment_a, second_a, gradients[:, :, :width_a]
    )
    updated_b, moment_b_new, second_b_new = adam_update(
        adapter_b, moment_b, second_b, gradients[:, :, width_a:]
    )
    fresh_a = updated_a.astype(jnp.bfloat16)
    fresh_b = updated_b.astype(jnp.bfloat16)
    requests = decode_inputs[0]
    request_tenants = request_adapter[0]
    group_now = lax.axis_index("group")
    slot_a, slot_b = (
        lax.all_gather(fresh_a, ("dp", "group"), axis=0, tiled=True),
        lax.all_gather(fresh_b, ("dp", "group"), axis=0, tiled=True),
    )
    slot_ids = jnp.arange(slot_a.shape[0], dtype=jnp.int32)
    served_flag = tenant_group[request_tenants] == group_now
    chosen = ((request_tenants[:, None] == slot_ids[None, :]) & served_flag[:, None]).astype(
        jnp.bfloat16
    )
    request_a = jnp.einsum(
        "qt,trd->qrd", chosen, slot_a, preferred_element_type=jnp.float32
    ).astype(jnp.bfloat16)
    request_up_weight = jnp.einsum(
        "qt,trk->qrk", chosen, slot_b, preferred_element_type=jnp.float32
    ).astype(jnp.bfloat16)
    tensor_index = lax.axis_index("tensor")
    x_slice = lax.dynamic_slice_in_dim(requests, tensor_index * width_a, width_a, 2)
    dec_part = jnp.einsum("qsd,qrd->qsr", x_slice, request_a, preferred_element_type=jnp.float32)
    dec_total = lax.psum(dec_part, "tensor")
    decode_input = dec_total.astype(jnp.bfloat16)
    frozen_output = jnp.einsum(
        "qsd,dk->qsk", requests, dec_weight, preferred_element_type=jnp.float32
    )
    adapter_delta = jnp.einsum(
        "fyd,fdb->fyb", decode_input, request_up_weight, preferred_element_type=jnp.float32
    )
    decode_output = (frozen_output + adapter_scale * adapter_delta).astype(jnp.bfloat16)[None]
    return (
        updated_a,
        updated_b,
        moment_a_new,
        moment_b_new,
        second_a_new,
        second_b_new,
        decode_output,
    )


def solution(mesh):
    return jax.shard_map(
        local,
        mesh=mesh,
        in_specs=(
            P(("dp", "group"), "tensor"),
            P(("dp", "group"), "tensor"),
            P(("dp", "group")),
            P(("dp", "group")),
            P(("dp", "group"), None, "tensor"),
            P(("dp", "group"), None, "tensor"),
            P(("dp", "group"), None, "tensor"),
            P(("dp", "group"), None, "tensor"),
            P(("dp", "group"), None, "tensor"),
            P(("dp", "group"), None, "tensor"),
            P(),
            P("group", "dp", None, None),
            P(None, "tensor"),
            P("group", "dp"),
        ),
        out_specs=(
            P(("dp", "group"), None, "tensor"),
            P(("dp", "group"), None, "tensor"),
            P(("dp", "group"), None, "tensor"),
            P(("dp", "group"), None, "tensor"),
            P(("dp", "group"), None, "tensor"),
            P(("dp", "group"), None, "tensor"),
            P("group", "dp", None, "tensor"),
        ),
        check_vma=False,
    )
```

profile of v0, /device:TPU:14, one launch (start us, length us, event | category | flops | bytes accessed | tf_op | source)
XLA Modules:
  0.0 533.2 jit_solution(379801501742972133)
XLA Ops:
  7.2 1.8 convert_element_type.63
  9.0 0.0 all-reduce.3.cloned.1.call-start
  9.1 0.8 convert_element_type.60
  9.8 52.2 %all_gather.12 = bf16[64,32,128]{2,1,0:T(8,128)(2,1)S(1)} all-gather(bf16[2,32,128]{2,1,0:T(8,128)(2,1)S(1)} %convert_element_type.60), channel_id=1, replica_groups=mesh['dp'=8,'group'=4,'tensor'=8] {'dp','group'}, dimensions={0}, use_global_device_ids=true | all-gather | bytes 540672 | tf_op jit(solution)/shard_map/all_gather | solution.py:54
  62.1 0.7 fusion.53
  62.8 1.0 convolution_convert_fusion.4
  63.7 1.9 convolution_convert_fusion.5
  65.7 28.4 %all-gather.3.cloned.1.call-done = bf16[64,32,1024]{2,1,0:T(8,128)(2,1)} async-done(((bf16[2,32,1024]{2,1,0:T(8,128)(2,1)}), bf16[64,32,1024]{2,1,0:T(8,128)(2,1)}) %all-gather.3.cloned.1.call-update) | async-done | bytes 4194320 | tf_op jit(solution)/shard_map/all_gather | solution.py:53
  94.1 6.7 %fusion.8 = bf16[8,32,1024]{2,0,1:T(8,128)(2,1)S(1)} fusion(bf16[64,32,1024]{2,1,0:T(8,128)(2,1)} %all-gather.3.cloned.1.call-done, s32[8]{0:T(128)} %param.16), kind=kOutput, calls=%fused_computation.13 | convolution fusion | flops 33817088 | bytes 4718624 | tf_op jit(solution)/shard_map/bt,trd->brd/dot_general | solution.py:59
  100.8 1.4 fusion.27
  102.2 0.2 reduce-scatter.2.cloned.1.call-start
  102.5 61.4 %all-reduce.3.cloned.1.call-done = (bf16[8,128,32]{1,2,0:T(8,128)(2,1)}, bf16[8,128,32]{1,2,0:T(8,128)(2,1)}) async-done(((bf16[8,128,32]{1,2,0:T(8,128)(2,1)}, bf16[8,128,32]{1,2,0:T(8,128)(2,1)}), (bf16[8,128,32]{1,2,0:T(8,128)(2,1)}, bf16[8,128,32]{1,2,0:T(8,128)(2,1)})) %all-reduce.3.cloned.1.call-update) | async-done | bytes 131088 | tf_op jit(solution)/shard_map/psum | solution.py:68
  163.9 1.2 convolution_multiply_fusion.1
  165.0 1.2 convolution_multiply_fusion
  166.3 0.1 pad_maximum_fusion
  166.4 4.3 convolution_convert_fusion.1
  170.7 4.8 copy.56
  175.5 0.0 all-gather.5.cloned.1.call-start
  175.6 223.9 %reduce-scatter.2.cloned.1.call-done = bf16[2,32,1152]{2,1,0:T(8,128)(2,1)} async-done(((bf16[64,32,1152]{2,1,0:T(8,128)(2,1)}), bf16[2,32,1152]{2,1,0:T(8,128)(2,1)}) %reduce-scatter.2.cloned.1.call-update) | async-done | bytes 147472 | tf_op jit(solution)/shard_map/reduce_scatter | solution.py:84
  399.5 0.9 convert_element_type.68
  400.5 1.0 fusion.62
  401.6 1.2 gather_fusion
  402.9 0.7 fusion.64
  403.5 47.9 %all_gather.15 = bf16[64,32,128]{2,1,0:T(8,128)(2,1)S(1)} all-gather(bf16[2,32,128]{2,1,0:T(8,128)(2,1)S(1)} %get-tuple-element.34), channel_id=1, replica_groups=mesh['dp'=8,'group'=4,'tensor'=8] {'dp','group'}, dimensions={0}, use_global_device_ids=true | all-gather | bytes 540672 | tf_op jit(solution)/shard_map/all_gather | solution.py:105
  451.4 0.5 convolution_convert_fusion.2
  451.9 29.5 %all-gather.5.cloned.1.call-done = bf16[64,32,1024]{2,1,0:T(8,128)(2,1)} async-done(((bf16[2,32,1024]{2,1,0:T(8,128)(2,1)}), bf16[64,32,1024]{2,1,0:T(8,128)(2,1)}) %all-gather.5.cloned.1.call-update) | async-done | bytes 4194320 | tf_op jit(solution)/shard_map/all_gather | solution.py:104
  481.4 8.5 %convolution_convert_fusion = bf16[128,32,1024]{2,0,1:T(8,128)(2,1)S(1)} fusion(bf16[64,32,1024]{2,1,0:T(8,128)(2,1)} %all-gather.5.cloned.1.call-done, s32[128]{0:T(128)S(1)} %bitcast.45, pred[128]{0:T(512)(128)(4,1)S(1)} %broadcast_compare_fusion), kind=kOutput, calls=%fused_computation.3 | convolution fusion | flops 541081600 | bytes 12583552 | tf_op jit(solution)/shard_map/qt,trd->qrd/dot_general | solution.py:112
  489.9 5.8 %fusion = f32[128,2,32]{2,1,0:T(2,128)S(1)} fusion(bf16[128,32,1024]{2,0,1:T(8,128)(2,1)S(1)} %convolution_convert_fusion, bf16[1,128,2,8192]{3,2,1,0:T(2,128)(2,1)} %param.25, s32[]{:T(128)S(6)} %select_n.13), kind=kOutput, calls=%fused_computation.1 | convolution fusion | flops 16777216 | bytes 8945668 | tf_op jit(solution)/shard_map/qsd,qrd->qsr/dot_general | solution.py:120
  495.7 21.9 %psum.23 = bf16[128,2,32]{2,1,0:T(2,128)(2,1)S(1)} all-reduce(f32[128,2,32]{2,1,0:T(2,128)S(1)} %fusion), channel_id=1, replica_groups=mesh['dp'=8,'group'=4,'tensor'=8] {'tensor'}, use_global_device_ids=true, to_apply=%region_3.0 | all-reduce | flops 8192 | bytes 49152 | tf_op jit(solution)/shard_map/psum | solution.py:121
  517.6 0.7 fusion.28
  518.3 7.6 %fusion.22 = bf16[1,128,2,128]{3,1,2,0:T(8,128)(2,1)S(1)} fusion(bf16[8192,128]{1,0:T(8,128)(2,1)} %param.26, bf16[128,2,8192]{2,1,0:T(2,128)(2,1)} %bitcast.46, f32[128,2,128]{2,1,0:T(2,128)S(1)} %fusion.28), kind=kOutput, calls=%fused_computation.22 | convolution fusion | flops 536969216 | bytes 6488064 | tf_op jit(solution)/shard_map/qsd,dk->qsk/dot_general | solution.py:123
  525.9 0.7 copy.63
  (30 shorter events, 0.2 us)
Async XLA Ops:
  7.2 93.6 %copy-start = (bf16[1024,1024]{1,0:T(8,128)(2,1)S(1)}, bf16[1024,1024]{1,0:T(8,128)(2,1)}, u32[]{:S(2)}) copy-start(bf16[1024,1024]{1,0:T(8,128)(2,1)} %param.14) | copy-start | bytes 6291460
  7.2 86.9 %all-gather.3.cloned.1.call-start = ((), (), s32[]{:S(2)}) async-start(), calls=%async_computation.1 | async-start | bytes 4325376 | tf_op jit(solution)/shard_map/all_gather | solution.py:53
  9.0 154.8 %all-reduce.3.cloned.1.call-start = ((), (), s32[]{:S(2)}) async-start(), calls=%async_computation.4 | async-start | bytes 262144 | tf_op jit(solution)/shard_map/psum | solution.py:68
  62.8 101.1 %copy-start.5 = (bf16[1024,128]{1,0:T(8,128)(2,1)S(1)}, bf16[1024,128]{1,0:T(8,128)(2,1)}, u32[]{:S(2)}) copy-start(bf16[1024,128]{1,0:T(8,128)(2,1)} %param.15) | copy-start | bytes 786436
  100.8 65.6 %copy-start.9 = (s32[8]{0:T(128)S(1)}, s32[8]{0:T(128)}, u32[]{:S(2)}) copy-start(s32[8]{0:T(128)} %param.16) | copy-start | bytes 100
  102.2 297.3 %reduce-scatter.2.cloned.1.call-start = ((), (), s32[]{:S(2)}) async-start(), calls=%async_computation.2 | async-start | bytes 4866048 | tf_op jit(solution)/shard_map/reduce_scatter | solution.py:84
  175.4 225.0 %copy-start.2 = (f32[2,32,1024]{2,1,0:T(8,128)S(1)}, f32[2,32,1024]{2,1,0:T(8,128)}, u32[]{:S(2)}) copy-start(f32[2,32,1024]{2,1,0:T(8,128)} %param.18) | copy-start | bytes 786436
  175.4 225.0 %copy-start.3 = (f32[2,32,1024]{2,1,0:T(8,128)S(1)}, f32[2,32,1024]{2,1,0:T(8,128)}, u32[]{:S(2)}) copy-start(f32[2,32,1024]{2,1,0:T(8,128)} %param.20) | copy-start | bytes 786436
  175.4 225.0 %copy-start.4 = (f32[2,32,1024]{2,1,0:T(8,128)S(1)}, f32[2,32,1024]{2,1,0:T(8,128)}, u32[]{:S(2)}) copy-start(f32[2,32,1024]{2,1,0:T(8,128)} %param.22) | copy-start | bytes 786436
  175.4 226.1 %copy-start.10 = (s32[1,128]{1,0:T(1,128)S(1)}, s32[1,128]{1,0:T(1,128)}, u32[]{:S(2)}) copy-start(s32[1,128]{1,0:T(1,128)} %param.27) | copy-start | bytes 1540
  175.5 226.1 %copy-start.1 = (s32[64]{0:T(128)S(1)}, s32[64]{0:T(128)}, u32[]{:S(2)}) copy-start(s32[64]{0:T(128)} %param.24) | copy-start | bytes 772
  175.5 227.4 %copy-start.6 = (f32[2,32,128]{2,1,0:T(8,128)S(1)}, f32[2,32,128]{2,1,0:T(8,128)}, u32[]{:S(2)}) copy-start(f32[2,32,128]{2,1,0:T(8,128)} %param.19) | copy-start | bytes 98308
  175.5 227.4 %copy-start.7 = (f32[2,32,128]{2,1,0:T(8,128)S(1)}, f32[2,32,128]{2,1,0:T(8,128)}, u32[]{:S(2)}) copy-start(f32[2,32,128]{2,1,0:T(8,128)} %param.21) | copy-start | bytes 98308
  175.5 227.4 %copy-start.8 = (f32[2,32,128]{2,1,0:T(8,128)S(1)}, f32[2,32,128]{2,1,0:T(8,128)}, u32[]{:S(2)}) copy-start(f32[2,32,128]{2,1,0:T(8,128)} %param.23) | copy-start | bytes 98308
  175.5 305.8 %all-gather.5.cloned.1.call-start = ((), (), s32[]{:S(2)}) async-start(), calls=%async_computation.3 | async-start | bytes 4325376 | tf_op jit(solution)/shard_map/all_gather | solution.py:104
Sparse Core Ops, SparseCore 0:
  11.2 82.8 all-gather.2
  102.4 61.4 all-reduce.2
  175.6 223.8 reduce-scatter.1
  402.3 79.0 all-gather.4
where the time goes:
time: 539 us; the launch traced here: 533 us
  waiting for transfers between devices  343 us (64%)
  blocking collectives  122 us (23%)
  matrix products  40.8 us (8%)
  between operations  14 us (3%)
  local copies, waits for them, and re-layouts  6.77 us (1%)
  other arithmetic  5.97 us (1%)
    reduce_scatter x1, waiting for transfers between devices, local(): lax.psum_scatter(jnp.einsum('tb,brw->trw', chosen, grad_blocks, precision...  224 us
    psum x1, waiting for transfers between devices, local(): lax.psum(in_part.astype(jnp.bfloat16), 'tensor').astype(jnp.float32)  61.4 us
    all_gather x1, blocking collectives, local(): piece_b = lax.all_gather(b_half, ('dp', 'group'), axis=0, tiled=True)  52.2 us
    all_gather x1, blocking collectives, local(): lax.all_gather(fresh_b, ('dp', 'group'), axis=0, tiled=True)  47.9 us
    all_gather x1, waiting for transfers between devices, local(): lax.all_gather(fresh_a, ('dp', 'group'), axis=0, tiled=True)  29.5 us
    all_gather x1, waiting for transfers between devices, local(): piece_a = lax.all_gather(a_half, ('dp', 'group'), axis=0, tiled=True)  28.4 us
    psum x1, blocking collectives, local(): dec_total = lax.psum(dec_part, 'tensor')  21.9 us
  transfers between devices with their start and end apart: 4, of which 4 were waited for; matrix products, arithmetic and copies ran while one was open for 1% of the time, Pallas kernels for 0%

commit v1 on v0

v1 whole, which is shorter than its diff:
```python
import functools

import jax
import jax.numpy as jnp
from jax import lax
from jax.experimental import pallas as pl
from jax.experimental.pallas import tpu as pltpu
from jax.sharding import PartitionSpec as P

STEP_NUM = 10

adapter_scale = 2.0
beta_one = 0.9
beta_two = 0.999
step_rate = 0.001
adam_eps = 1e-08

BF = jnp.bfloat16
F32 = jnp.float32
VMEM_LIMIT = 40 * 1024 * 1024


def dot(a, b, dims):
    return lax.dot_general(a, b, (dims, ((), ())), preferred_element_type=F32)


def shift(x, axis, distance):
    size = lax.axis_size(axis)
    return lax.ppermute(x, axis, [(i, (i + distance) % size) for i in range(size)])


def spread(x, axis):
    return [x] + [shift(x, axis, d) for d in range(1, lax.axis_size(axis))]


def vmem(n):
    return [pl.BlockSpec(memory_space=pltpu.VMEM)] * n


def smem(n):
    return [pl.BlockSpec(memory_space=pltpu.SMEM)] * n


PARAMS = pltpu.CompilerParams(vmem_limit_bytes=VMEM_LIMIT)


def pack_kernel(source, count, x_ref, dy_ref, *outs):
    step = pl.program_id(0)
    rows, width = x_ref.shape
    live = lax.broadcasted_iota(jnp.int32, dy_ref.shape, 0) < count[source[step]]
    dy = jnp.where(live, dy_ref[...].astype(F32), 0.0).astype(BF)
    for d, out in enumerate(outs):

        @pl.when(step // 2 == d)
        def _():
            out[:, :width] = x_ref[...]
            out[:, width:] = dy


def pack(source, count, learn_x, learn_dy, groups):
    blocks = source.shape[0]
    rows = learn_x.shape[0] // blocks
    width, width_b = learn_x.shape[1], learn_dy.shape[1]
    each = blocks // groups
    return pl.pallas_call(
        pack_kernel,
        grid_spec=pltpu.PrefetchScalarGridSpec(
            num_scalar_prefetch=2,
            grid=(blocks,),
            in_specs=[
                pl.BlockSpec((rows, width), lambda s, source, count: (source[s], 0)),
                pl.BlockSpec((rows, width_b), lambda s, source, count: (source[s], 0)),
            ],
            out_specs=[
                pl.BlockSpec(
                    (rows, width + width_b),
                    lambda s, source, count, d=d: (jnp.clip(s - each * d, 0, each - 1), 0),
                )
                for d in range(groups)
            ],
        ),
        out_shape=[jax.ShapeDtypeStruct((each * rows, width + width_b), BF)] * groups,
        compiler_params=PARAMS,
    )(source, count, learn_x, learn_dy)


def low_kernel(rank, rows, index, *refs):
    *refs, out, table = refs
    adapters, blocks = refs[:8], refs[8:]
    wide = blocks[0].shape[1]
    width = wide - 128
    for d, ref in enumerate(adapters):
        for j in range(2):
            table[2 * d + j] = ref[j * rank : (j + 1) * rank, :]
    for s in range(2 * len(blocks)):
        ref = blocks[s // 2]
        part = pl.ds((s % 2) * rows, rows)
        chosen = table[index[s]]
        low_in = dot(chosen[:, :width], ref[part, :width], ((1,), (1,)))
        low_back = dot(chosen[:, width:], ref[part, width:], ((1,), (1,)))
        out[s * 2 * rank : s * 2 * rank + rank, :] = low_in.astype(BF)
        out[s * 2 * rank + rank : (s + 1) * 2 * rank, :] = low_back.astype(BF)


def low(index, adapters, blocks, rank):
    rows = blocks[0].shape[0] // 2
    wide = blocks[0].shape[1]
    return pl.pallas_call(
        functools.partial(low_kernel, rank, rows),
        in_specs=smem(1) + vmem(len(adapters) + len(blocks)),
        out_specs=pl.BlockSpec(memory_space=pltpu.VMEM),
        out_shape=jax.ShapeDtypeStruct((2 * len(blocks) * 2 * rank, rows), BF),
        scratch_shapes=[pltpu.VMEM((2 * len(adapters), rank, wide), BF)],
        compiler_params=PARAMS,
    )(index, *adapters, *blocks)


def grad_kernel(rank, rows, parts, groups, index, *refs):
    lows, blocks = refs[:parts], refs[parts : parts + groups]
    outs, sums = refs[parts + groups : -1], refs[-1]
    wide = blocks[0].shape[1]
    width = wide - 128
    total = lows[0][...].astype(F32)
    for ref in lows[1:]:
        total = total + ref[...].astype(F32)
    total = total.astype(BF)
    sums[...] = jnp.zeros_like(sums)
    for s in range(2 * groups):
        ref = blocks[s // 2]
        part = pl.ds((s % 2) * rows, rows)
        low_in = total[s * 2 * rank : s * 2 * rank + rank]
        low_back = total[s * 2 * rank + rank : (s + 1) * 2 * rank]
        here = index[s]
        sums[here, :, :width] += dot(low_back, ref[part, :width], ((1,), (0,)))
        sums[here, :, width:] += dot(low_in, ref[part, width:], ((1,), (0,)))
    for d, out in enumerate(outs):
        for j in range(2):
            out[j * rank : (j + 1) * rank, :] = (adapter_scale * sums[2 * d + j]).astype(BF)


def grad(index, lows, blocks, rank, targets):
    rows = blocks[0].shape[0] // 2
    wide = blocks[0].shape[1]
    return pl.pallas_call(
        functools.partial(grad_kernel, rank, rows, len(lows), len(blocks)),
        in_specs=smem(1) + vmem(len(lows) + len(blocks)),
        out_specs=vmem(targets),
        out_shape=[jax.ShapeDtypeStruct((2 * rank, wide), BF)] * targets,
        scratch_shapes=[pltpu.VMEM((2 * targets, rank, wide), F32)],
        compiler_params=PARAMS,
    )(index, *lows, *blocks)


def adam_update(weights, moment, second, gradient):
    moment_new = beta_one * moment + (1.0 - beta_one) * gradient
    second_new = beta_two * second + (1.0 - beta_two) * gradient * gradient
    unbiased_m = moment_new / (1.0 - beta_one**STEP_NUM)
    unbiased_v = second_new / (1.0 - beta_two**STEP_NUM)
    weights_new = weights - step_rate * unbiased_m / (jnp.sqrt(unbiased_v) + adam_eps)
    return (weights_new, moment_new, second_new)


def adam_kernel(parts, *refs):
    grads, refs = refs[:parts], refs[parts:]
    state_a, state_b = refs[0:3], refs[3:6]
    new_a, new_b, fresh = refs[6:9], refs[9:12], refs[12]
    width = state_a[0].shape[1]
    total = grads[0][...].astype(F32)
    for ref in grads[1:]:
        total = total + ref[...].astype(F32)
    for state, new, cols in (
        (state_a, new_a, slice(0, width)),
        (state_b, new_b, slice(width, None)),
    ):
        values = adam_update(*[ref[...] for ref in state], total[:, cols])
        for ref, value in zip(new, values):
            ref[...] = value
        fresh[:, cols] = values[0].astype(BF)


def adam(grads, state_a, state_b):
    rows, width = state_a[0].shape
    width_b = state_b[0].shape[1]
    wide = width + width_b
    tile = 16
    steps = rows // tile

    def spec(w):
        return pl.BlockSpec((tile, w), lambda i: (i, 0))

    return pl.pallas_call(
        functools.partial(adam_kernel, len(grads)),
        grid=(steps,),
        in_specs=[spec(wide)] * len(grads) + [spec(width)] * 3 + [spec(width_b)] * 3,
        out_specs=[spec(width)] * 3 + [spec(width_b)] * 3 + [spec(wide)],
        out_shape=[jax.ShapeDtypeStruct((rows, width), F32)] * 3
        + [jax.ShapeDtypeStruct((rows, width_b), F32)] * 3
        + [jax.ShapeDtypeStruct((rows, wide), BF)],
        compiler_params=PARAMS,
    )(*grads, *state_a, *state_b)


def pick_kernel(rank, index, *refs):
    *refs, out = refs
    for i in range(2):
        device, slot = index[i] // 2, index[i] % 2
        for d, ref in enumerate(refs):

            @pl.when(device == d)
            def _():
                out[i * rank : (i + 1) * rank, :] = ref[
                    pl.ds(pl.multiple_of(slot * rank, rank), rank), :
                ]


def pick(index, arrays, rank):
    return pl.pallas_call(
        functools.partial(pick_kernel, rank),
        in_specs=smem(1) + vmem(len(arrays)),
        out_specs=pl.BlockSpec(memory_space=pltpu.VMEM),
        out_shape=jax.ShapeDtypeStruct(arrays[0].shape, BF),
        compiler_params=PARAMS,
    )(index, *arrays)


def decode_in_kernel(rank, slots, x, *refs):
    *refs, out = refs
    width = x.shape[1]
    total = jnp.zeros(out.shape, F32)
    for d, ref in enumerate(refs):
        both = dot(ref[:, :width], x[...], ((1,), (1,)))
        for j in range(2):
            total += jnp.where(slots[...] == 2 * d + j, both[j * rank : (j + 1) * rank], 0.0)
    out[...] = total


def decode_in(slots, x, fresh, rank):
    return pl.pallas_call(
        functools.partial(decode_in_kernel, rank),
        in_specs=vmem(2 + len(fresh)),
        out_specs=pl.BlockSpec(memory_space=pltpu.VMEM),
        out_shape=jax.ShapeDtypeStruct((rank, x.shape[0]), F32),
        compiler_params=PARAMS,
    )(slots, x, *fresh)


def decode_out_kernel(rank, parts, slots, frozen, *refs):
    lows, fresh, out = refs[:parts], refs[parts:-1], refs[-1]
    width_b = frozen.shape[1]
    total = lows[0][...]
    for ref in lows[1:]:
        total = total + ref[...]
    total = total.astype(BF).astype(F32)
    result = jnp.zeros(frozen.shape, F32)
    for d, ref in enumerate(fresh):
        both = jnp.concatenate(
            [jnp.where(slots[...] == 2 * d + j, total, 0.0) for j in range(2)], axis=0
        )
        result += dot(both.T.astype(BF), ref[...], ((1,), (0,)))
    out[...] = (frozen[...] + adapter_scale * result).astype(BF)


def decode_out(slots, frozen, lows, fresh, rank):
    width_b = frozen.shape[1]
    wide = fresh[0].shape[1]
    whole = [pl.BlockSpec(a.shape, lambda i: (0, 0)) for a in (slots, frozen, *lows)]
    ends = [
        pl.BlockSpec((2 * rank, width_b), lambda i: (0, wide // width_b - 1)) for _ in fresh
    ]
    return pl.pallas_call(
        functools.partial(decode_out_kernel, rank, len(lows)),
        grid=(1,),
        in_specs=whole + ends,
        out_specs=pl.BlockSpec(frozen.shape, lambda i: (0, 0)),
        out_shape=jax.ShapeDtypeStruct(frozen.shape, BF),
        compiler_params=PARAMS,
    )(slots, frozen, *lows, *fresh)


def column_of(tenant, groups):
    return (tenant // 2) % groups


def local(
    learn_x,
    learn_dy,
    block_tenant,
    block_count,
    adapter_a,
    adapter_b,
    moment_a,
    moment_b,
    second_a,
    second_b,
    tenant_group,
    decode_inputs,
    dec_weight,
    request_adapter,
):
    groups = lax.axis_size("group")
    rows_dp = lax.axis_size("dp")
    group = lax.axis_index("group")
    row = lax.axis_index("dp")
    owned, rank, width = adapter_a.shape
    width_b = adapter_b.shape[2]
    span = groups * owned

    def flat(x):
        return x.reshape(owned * rank, x.shape[2])

    own = jnp.concatenate([flat(adapter_a), flat(adapter_b)], axis=1).astype(BF)
    table = spread(own, "dp")

    blocks = block_tenant.shape[0]
    column = column_of(block_tenant, groups)
    distance = (column - group) % groups
    earlier = jnp.tril(distance[:, None] == distance[None, :], -1).astype(jnp.int32)
    place = distance * (blocks // groups) + jnp.sum(earlier, axis=1)
    here = place[None, :] == jnp.arange(blocks, dtype=jnp.int32)[:, None]
    source = jnp.sum(
        jnp.where(here, jnp.arange(blocks, dtype=jnp.int32)[None, :], 0), axis=1, dtype=jnp.int32
    )
    packed = pack(source, block_count, learn_x, learn_dy, groups)
    tenants = jnp.sum(jnp.where(here, block_tenant[None, :], 0), axis=1, dtype=jnp.int32)
    tenants = tenants.reshape(groups, blocks // groups)
    arrived = [packed[0]] + [shift(packed[d], "group", d) for d in range(1, groups)]
    tenants = jnp.concatenate(
        [tenants[0]] + [shift(tenants[d], "group", d) for d in range(1, groups)]
    )
    tenant_row, tenant_slot = tenants // span, tenants % owned

    partial = low(((row - tenant_row) % rows_dp) * owned + tenant_slot, table, arrived, rank)
    tensor_size = lax.axis_size("tensor")
    lows = [partial] + [
        lax.ppermute(partial, "tensor", [(i, i ^ d) for i in range(tensor_size)])
        for d in range(1, tensor_size)
    ]
    sums = grad(
        ((tenant_row - row) % rows_dp) * owned + tenant_slot, lows, arrived, rank, rows_dp
    )
    pieces = [sums[0]] + [shift(sums[d], "dp", d) for d in range(1, rows_dp)]
    *new, fresh = adam(
        pieces,
        [flat(x) for x in (adapter_a, moment_a, second_a)],
        [flat(x) for x in (adapter_b, moment_b, second_b)],
    )

    in_row = spread(fresh, "group")
    tenant_ids = jnp.arange(tenant_group.shape[0], dtype=jnp.int32)
    served = (tenant_group == group).astype(jnp.int32)
    by_row = served.reshape(rows_dp, span)
    slot_of = jnp.cumsum(by_row, axis=1) - by_row
    mine = lax.dynamic_slice_in_dim(by_row, row, 1, 0)[0]
    mine_slot = lax.dynamic_slice_in_dim(slot_of, row, 1, 0)[0]
    position = jnp.arange(span, dtype=jnp.int32)
    relative = ((group - position // owned) % groups) * owned + position % owned
    wanted = jnp.sum(
        jnp.where(
            (mine[None, :] == 1)
            & (mine_slot[None, :] == jnp.arange(owned, dtype=jnp.int32)[:, None]),
            relative[None, :],
            0,
        ),
        axis=1,
        dtype=jnp.int32,
    )
    served_fresh = spread(pick(wanted, in_row, rank), "dp")

    slot_here = ((row - tenant_ids // span) % rows_dp) * owned + slot_of.reshape(-1)
    slot_here = jnp.where(served == 1, slot_here, -1)
    request_slot = jnp.sum(
        jnp.where(request_adapter[0][:, None] == tenant_ids[None, :], slot_here[None, :], 0),
        axis=1,
        dtype=jnp.int32,
    )
    requests = decode_inputs[0]
    steps = requests.shape[1]
    count = requests.shape[0] * steps
    slots = jnp.broadcast_to(request_slot[:, None], (requests.shape[0], steps)).reshape(1, count)
    frozen = jnp.einsum("qsd,dk->qsk", requests, dec_weight, preferred_element_type=F32)
    frozen = frozen.reshape(count, width_b)
    x_slice = lax.dynamic_slice_in_dim(requests, lax.axis_index("tensor") * width, width, 2)
    dec_part = decode_in(slots, x_slice.reshape(count, width), served_fresh, rank)
    dec_parts = [dec_part] + [
        lax.ppermute(dec_part, "tensor", [(i, i ^ d) for i in range(tensor_size)])
        for d in range(1, tensor_size)
    ]
    decoded = decode_out(slots, frozen, dec_parts, served_fresh, rank)
    new_a = [x.reshape(adapter_a.shape) for x in new[:3]]
    new_b = [x.reshape(adapter_b.shape) for x in new[3:]]
    return (
        new_a[0],
        new_b[0],
        new_a[1],
        new_b[1],
        new_a[2],
        new_b[2],
        decoded.reshape((1,) + requests.shape[:2] + (width_b,)),
    )


def solution(mesh):
    state = P(("dp", "group"), None, "tensor")
    return jax.shard_map(
        local,
        mesh=mesh,
        in_specs=(
            P(("dp", "group"), "tensor"),
            P(("dp", "group"), "tensor"),
            P(("dp", "group")),
            P(("dp", "group")),
            state,
            state,
            state,
            state,
            state,
            state,
            P(),
            P("group", "dp", None, None),
            P(None, "tensor"),
            P("group", "dp"),
        ),
        out_specs=(
            state,
            state,
            state,
            state,
            state,
            state,
            P("group", "dp", None, "tensor"),
        ),
        check_vma=False,
    )
```

time: 539 us -> 240 us (0.45)
  waiting for transfers between devices: 343 us -> 110 us
  blocking collectives: 122 us -> 0 us
  starting transfers between devices: 0.34 us -> 72 us
  matrix products: 40.8 us -> 3.5 us
  local copies, waits for them, and re-layouts: 6.77 us -> 26.3 us
  Pallas kernels: 0 us -> 15.1 us
  between operations: 14 us -> 0.87 us
    reduce_scatter x1 -> x0, waiting for transfers between devices: 224 us -> none  [local(): lax.psum_scatter(jnp.einsum('tb,brw->trw', chosen, grad_blocks, precision...]
    ppermute x0 -> x44, waiting for transfers between devices: none -> 110 us  [the longest x30 98.1 us: shift(): lax.ppermute(x, axis, [(i, (i + distance) % size) for i in range(size)])]
    all_gather x2 -> x0, blocking collectives: 100 us -> none  [the longest x1 52.2 us: local(): piece_b = lax.all_gather(b_half, ('dp', 'group'), axis=0, tiled=True)]
    ppermute x0 -> x44, starting transfers between devices: none -> 72 us  [the longest x30 58 us: shift(): lax.ppermute(x, axis, [(i, (i + distance) % size) for i in range(size)])]
    psum x1 -> x0, waiting for transfers between devices: 61.4 us -> none  [local(): lax.psum(in_part.astype(jnp.bfloat16), 'tensor').astype(jnp.float32)]
    all_gather x2 -> x0, waiting for transfers between devices: 57.9 us -> none  [the longest x1 29.5 us: local(): lax.all_gather(fresh_a, ('dp', 'group'), axis=0, tiled=True)]
    dot_general x12 -> x1, matrix products: 40.8 us -> 3.5 us  [local(): jnp.einsum('qsd,dk->qsk', requests, dec_weight, preferred_element_type=F32)]
    psum x1 -> x0, blocking collectives: 21.9 us -> none  [local(): dec_total = lax.psum(dec_part, 'tensor')]
  transfers between devices with their start and end apart: 4 -> 44, of which waited for: 4 -> 25; matrix products, arithmetic and copies ran while one was open for 1% -> 8% of each run, Pallas kernels for 0% -> 1%
where the time goes in v1:
time: 240 us; the launch traced here: 235 us
  waiting for transfers between devices  110 us (46%)
  starting transfers between devices  72 us (30%)
  local copies, waits for them, and re-layouts  26.3 us (11%)
  Pallas kernels  15.1 us (6%)
  other arithmetic  7.16 us (3%)
  matrix products  3.5 us (1%)
    ppermute x30, waiting for transfers between devices, shift(): lax.ppermute(x, axis, [(i, (i + distance) % size) for i in range(size)])  98.1 us
    ppermute x30, starting transfers between devices, shift(): lax.ppermute(x, axis, [(i, (i + distance) % size) for i in range(size)])  58 us
    unnamed x42, local copies, waits for them, and re-layouts  15.2 us
    ppermute x7, waiting for transfers between devices, local(): lax.ppermute(partial, 'tensor', [(i, i ^ d) for i in range(tensor_size)])  12 us
    dot_general x1, local copies, waits for them, and re-layouts, local(): jnp.einsum('qsd,dk->qsk', requests, dec_weight, preferred_element_type=F32)  7.2 us
    ppermute x7, starting transfers between devices, local(): lax.ppermute(partial, 'tensor', [(i, i ^ d) for i in range(tensor_size)])  6.97 us
    ppermute x7, starting transfers between devices, local(): lax.ppermute(dec_part, 'tensor', [(i, i ^ d) for i in range(tensor_size)])  6.97 us
  transfers between devices with their start and end apart: 44, of which 25 were waited for; matrix products, arithmetic and copies ran while one was open for 8% of the time, Pallas kernels for 1%

profile of v1, /device:TPU:14, one launch (start us, length us, event | category | flops | bytes accessed | tf_op | source)
XLA Modules:
  0.0 235.1 jit_solution(12264616622927259989)
XLA Ops:
  10.0 3.5 %shard_map.189 = (bf16[256,1152]{1,0:T(8,128)(2,1)S(1)}, bf16[256,1152]{1,0:T(8,128)(2,1)}, bf16[256,1152]{1,0:T(8,128)(2,1)}, bf16[256,1152]{1,0:T(8,128)(2,1)}) custom-call(s32[8]{0:T(128)S(1)} %get-tuple-element.45.source, s32[8]{0:T(128)S(1)} %copy-done.19, bf16[1024,1024]{1,0:T(8,128)(2,1)S(1)} %copy-done.1, bf16[1024,128]{1,0:T(8,128)(2,1)S(1)} %copy-done.3), custom_call_target="tpu_custom_call" | custom-call | tf_op jit(solution)/shard_map/pallas_call | solution.py:65
  14.0 2.4 %collective-permute-start.11 = (bf16[256,1152]{1,0:T(8,128)(2,1)}, bf16[256,1152]{1,0:T(8,128)(2,1)}, u32[]{:S(2)}, u32[]{:S(2)}) collective-permute-start(bf16[256,1152]{1,0:T(8,128)(2,1)} %get-tuple-element.28), channel_id=1, source_target_pairs={{0,16},{8,24},{16,0},{24,8},{1,17},{9,25},{17,1},{25,9},{2,18},{10... | collective-permute-start | bytes 1769480 | tf_op jit(solution)/shard_map/ppermute | solution.py:29
  17.5 25.4 %collective-permute-done.2 = s32[2]{0:T(128)S(1)} collective-permute-done((s32[2]{0:T(128)S(1)}, s32[2]{0:T(128)S(1)}, u32[]{:S(2)}, u32[]{:S(2)}) %collective-permute-start.2) | collective-permute-done | bytes 40 | tf_op jit(solution)/shard_map/ppermute | solution.py:29
  44.7 3.3 %collective-permute-done.1 = s32[2]{0:T(128)S(1)} collective-permute-done((s32[2]{0:T(128)S(1)}, s32[2]{0:T(128)S(1)}, u32[]{:S(2)}, u32[]{:S(2)}) %collective-permute-start.1) | collective-permute-done | bytes 40 | tf_op jit(solution)/shard_map/ppermute | solution.py:29
  48.6 3.0 %collective-permute-done = s32[2]{0:T(128)} collective-permute-done((s32[2]{0:T(128)S(1)}, s32[2]{0:T(128)}, u32[]{:S(2)}, u32[]{:S(2)}) %collective-permute-start) | collective-permute-done | bytes 40 | tf_op jit(solution)/shard_map/ppermute | solution.py:29
  51.6 3.3 %collective-permute-start.4 = (bf16[64,1152]{1,0:T(8,128)(2,1)}, bf16[64,1152]{1,0:T(8,128)(2,1)S(1)}, u32[]{:S(2)}, u32[]{:S(2)}) collective-permute-start(bf16[64,1152]{1,0:T(8,128)(2,1)} %pad_maximum_fusion.refs_0_), channel_id=1, source_target_pairs={{0,64},{32,96},{64,128},{96,160},{128,192},{160,224},{192,0},{224,... | collective-permute-start | bytes 442376 | tf_op jit(solution)/shard_map/ppermute | solution.py:29
  54.9 4.0 %collective-permute-start.5 = (bf16[64,1152]{1,0:T(8,128)(2,1)}, bf16[64,1152]{1,0:T(8,128)(2,1)S(1)}, u32[]{:S(2)}, u32[]{:S(2)}) collective-permute-start(bf16[64,1152]{1,0:T(8,128)(2,1)} %pad_maximum_fusion.refs_0_), channel_id=1, source_target_pairs={{0,96},{32,128},{64,160},{96,192},{128,224},{160,0},{192,32},{224,... | collective-permute-start | bytes 442376 | tf_op jit(solution)/shard_map/ppermute | solution.py:29
  58.9 7.2 %collective-permute-done.4.refs_2_ = bf16[64,1152]{1,0:T(8,128)(2,1)S(1)} collective-permute-done((bf16[64,1152]{1,0:T(8,128)(2,1)}, bf16[64,1152]{1,0:T(8,128)(2,1)S(1)}, u32[]{:S(2)}, u32[]{:S(2)}) %collective-permute-start.4) | collective-permute-done | bytes 147488 | tf_op jit(solution)/shard_map/ppermute | solution.py:29
  66.8 9.0 %collective-permute-start.6 = (bf16[64,1152]{1,0:T(8,128)(2,1)}, bf16[64,1152]{1,0:T(8,128)(2,1)S(1)}, u32[]{:S(2)}, u32[]{:S(2)}) collective-permute-start(bf16[64,1152]{1,0:T(8,128)(2,1)} %pad_maximum_fusion.refs_0_), channel_id=1, source_target_pairs={{0,128},{32,160},{64,192},{96,224},{128,0},{160,32},{192,64},{224,... | collective-permute-start | bytes 442376 | tf_op jit(solution)/shard_map/ppermute | solution.py:29
  76.4 3.7 %collective-permute-start.7 = (bf16[64,1152]{1,0:T(8,128)(2,1)}, bf16[64,1152]{1,0:T(8,128)(2,1)S(1)}, u32[]{:S(2)}, u32[]{:S(2)}) collective-permute-start(bf16[64,1152]{1,0:T(8,128)(2,1)} %pad_maximum_fusion.refs_0_), channel_id=1, source_target_pairs={{0,160},{32,192},{64,224},{96,0},{128,32},{160,64},{192,96},{224,1... | collective-permute-start | bytes 442376 | tf_op jit(solution)/shard_map/ppermute | solution.py:29
  82.6 8.4 %collective-permute-done.7.refs_5_ = bf16[64,1152]{1,0:T(8,128)(2,1)S(1)} collective-permute-done((bf16[64,1152]{1,0:T(8,128)(2,1)}, bf16[64,1152]{1,0:T(8,128)(2,1)S(1)}, u32[]{:S(2)}, u32[]{:S(2)}) %collective-permute-start.7) | collective-permute-done | bytes 147488 | tf_op jit(solution)/shard_map/ppermute | solution.py:29
  92.7 4.4 %collective-permute-done.9.refs_7_ = bf16[64,1152]{1,0:T(8,128)(2,1)} collective-permute-done((bf16[64,1152]{1,0:T(8,128)(2,1)}, bf16[64,1152]{1,0:T(8,128)(2,1)}, u32[]{:S(2)}, u32[]{:S(2)}) %collective-permute-start.9) | collective-permute-done | bytes 147488 | tf_op jit(solution)/shard_map/ppermute | solution.py:29
  100.8 2.5 %shard_map.190.refs_0_ = bf16[512,128]{1,0:T(8,128)(2,1)S(1)} custom-call(s32[8]{0:T(128)S(1)} %get-tuple-element.47.index, bf16[64,1152]{1,0:T(8,128)(2,1)} %pad_maximum_fusion.refs_0_, bf16[64,1152]{1,0:T(8,128)(2,1)} %collective-permute-done.3.refs_1_, bf16[64,1152]{1,0:T(8,128)(2,1)S(1)} %copy-done.9, bf16[64,1152]{1,0:T(8,128)(2,1)S(1)} %copy-done.11, ...), custom_call_target="tpu_custom_call" | custom-call | tf_op jit(solution)/shard_map/pallas_call | solution.py:108
  111.7 4.9 %collective-permute-done.16.refs_4_ = bf16[512,128]{1,0:T(8,128)(2,1)S(1)} collective-permute-done((bf16[512,128]{1,0:T(8,128)(2,1)S(1)}, bf16[512,128]{1,0:T(8,128)(2,1)S(1)}, u32[]{:S(2)}, u32[]{:S(2)}) %collective-permute-start.16) | collective-permute-done | bytes 131104 | tf_op jit(solution)/shard_map/ppermute | solution.py:335
  122.3 2.8 %shard_map.191 = (bf16[64,1152]{1,0:T(8,128)(2,1)S(1)}, bf16[64,1152]{1,0:T(8,128)(2,1)S(1)}, bf16[64,1152]{1,0:T(8,128)(2,1)S(1)}, bf16[64,1152]{1,0:T(8,128)(2...) custom-call(s32[8]{0:T(128)S(1)} %fusion.8.index, ...), custom_call_target="tpu_custom_call" | custom-call | tf_op jit(solution)/shard_map/pallas_call | solution.py:144
  125.7 3.4 %collective-permute-start.21 = (bf16[64,1152]{1,0:T(8,128)(2,1)S(1)}, bf16[64,1152]{1,0:T(8,128)(2,1)S(1)}, u32[]{:S(2)}, u32[]{:S(2)}) collective-permute-start(bf16[64,1152]{1,0:T(8,128)(2,1)S(1)} %get-tuple-element.32), channel_id=1, source_target_pairs={{0,64},{32,96},{64,128},{96,160},{128,192},{160,224},{192,0},{224,... | collective-permute-start | bytes 442376 | tf_op jit(solution)/shard_map/ppermute | solution.py:29
  132.3 3.8 %collective-permute-start.24 = (bf16[64,1152]{1,0:T(8,128)(2,1)}, bf16[64,1152]{1,0:T(8,128)(2,1)S(1)}, u32[]{:S(2)}, u32[]{:S(2)}) collective-permute-start(bf16[64,1152]{1,0:T(8,128)(2,1)} %get-tuple-element.35), channel_id=1, source_target_pairs={{0,160},{32,192},{64,224},{96,0},{128,32},{160,64},{192,96},{224,1... | collective-permute-start | bytes 442376 | tf_op jit(solution)/shard_map/ppermute | solution.py:29
  136.2 3.1 %collective-permute-start.25 = (bf16[64,1152]{1,0:T(8,128)(2,1)}, bf16[64,1152]{1,0:T(8,128)(2,1)S(1)}, u32[]{:S(2)}, u32[]{:S(2)}) collective-permute-start(bf16[64,1152]{1,0:T(8,128)(2,1)} %get-tuple-element.36), channel_id=1, source_target_pairs={{0,192},{32,224},{64,0},{96,32},{128,64},{160,96},{192,128},{224,1... | collective-permute-start | bytes 442376 | tf_op jit(solution)/shard_map/ppermute | solution.py:29
  139.2 4.1 %collective-permute-done.21.refs_2_ = bf16[64,1152]{1,0:T(8,128)(2,1)S(1)} collective-permute-done((bf16[64,1152]{1,0:T(8,128)(2,1)S(1)}, bf16[64,1152]{1,0:T(8,128)(2,1)S(1)}, u32[]{:S(2)}, u32[]{:S(2)}) %collective-permute-start.21) | collective-permute-done | bytes 147488 | tf_op jit(solution)/shard_map/ppermute | solution.py:29
  144.1 5.9 %collective-permute-done.22.refs_3_ = bf16[64,1152]{1,0:T(8,128)(2,1)S(1)} collective-permute-done((bf16[64,1152]{1,0:T(8,128)(2,1)}, bf16[64,1152]{1,0:T(8,128)(2,1)S(1)}, u32[]{:S(2)}, u32[]{:S(2)}) %collective-permute-start.22) | collective-permute-done | bytes 147488 | tf_op jit(solution)/shard_map/ppermute | solution.py:29
  152.9 6.4 %collective-permute-done.25.refs_6_ = bf16[64,1152]{1,0:T(8,128)(2,1)S(1)} collective-permute-done((bf16[64,1152]{1,0:T(8,128)(2,1)}, bf16[64,1152]{1,0:T(8,128)(2,1)S(1)}, u32[]{:S(2)}, u32[]{:S(2)}) %collective-permute-start.25) | collective-permute-done | bytes 147488 | tf_op jit(solution)/shard_map/ppermute | solution.py:29
  170.9 3.5 %collective-permute-done.27.refs_1_ = bf16[64,1152]{1,0:T(8,128)(2,1)S(1)} collective-permute-done((bf16[64,1152]{1,0:T(8,128)(2,1)S(1)}, bf16[64,1152]{1,0:T(8,128)(2,1)S(1)}, u32[]{:S(2)}, u32[]{:S(2)}) %collective-permute-start.27) | collective-permute-done | bytes 147488 | tf_op jit(solution)/shard_map/ppermute | solution.py:29
  178.2 2.7 %collective-permute-start.30 = (bf16[64,1152]{1,0:T(8,128)(2,1)S(1)}, bf16[64,1152]{1,0:T(8,128)(2,1)S(1)}, u32[]{:S(2)}, u32[]{:S(2)}) collective-permute-start(bf16[64,1152]{1,0:T(8,128)(2,1)S(1)} %shard_map.193.refs_0_.refs_8_), channel_id=1, source_target_pairs={{0,32},{32,64},{64,96},{96,128},{128,160},{160,192},{192,224},{224... | collective-permute-start | bytes 442376 | tf_op jit(solution)/shard_map/ppermute | solution.py:29
  183.0 4.6 %collective-permute-start.33 = (bf16[64,1152]{1,0:T(8,128)(2,1)S(1)}, bf16[64,1152]{1,0:T(8,128)(2,1)S(1)}, u32[]{:S(2)}, u32[]{:S(2)}) collective-permute-start(bf16[64,1152]{1,0:T(8,128)(2,1)S(1)} %shard_map.193.refs_0_.refs_8_), channel_id=1, source_target_pairs={{0,128},{32,160},{64,192},{96,224},{128,0},{160,32},{192,64},{224,... | collective-permute-start | bytes 442376 | tf_op jit(solution)/shard_map/ppermute | solution.py:29
  187.6 3.5 %collective-permute-start.34 = (bf16[64,1152]{1,0:T(8,128)(2,1)S(1)}, bf16[64,1152]{1,0:T(8,128)(2,1)S(1)}, u32[]{:S(2)}, u32[]{:S(2)}) collective-permute-start(bf16[64,1152]{1,0:T(8,128)(2,1)S(1)} %shard_map.193.refs_0_.refs_8_), channel_id=1, source_target_pairs={{0,160},{32,192},{64,224},{96,0},{128,32},{160,64},{192,96},{224,1... | collective-permute-start | bytes 442376 | tf_op jit(solution)/shard_map/ppermute | solution.py:29
  192.1 7.1 %collective-permute-done.31.refs_2_.refs_10_ = bf16[64,1152]{1,0:T(8,128)(2,1)S(1)} collective-permute-done((bf16[64,1152]{1,0:T(8,128)(2,1)S(1)}, bf16[64,1152]{1,0:T(8,128)(2,1)S(1)}, u32[]{:S(2)}, u32[]{:S(2)}) %collective-permute-start.31) | collective-permute-done | bytes 147488 | tf_op jit(solution)/shard_map/ppermute | solution.py:29
  203.6 3.6 %collective-permute-done.33.refs_4_.refs_12_ = bf16[64,1152]{1,0:T(8,128)(2,1)S(1)} collective-permute-done((bf16[64,1152]{1,0:T(8,128)(2,1)S(1)}, bf16[64,1152]{1,0:T(8,128)(2,1)S(1)}, u32[]{:S(2)}, u32[]{:S(2)}) %collective-permute-start.33) | collective-permute-done | bytes 147488 | tf_op jit(solution)/shard_map/ppermute | solution.py:29
  207.2 4.8 %collective-permute-done.35.refs_6_.refs_14_ = bf16[64,1152]{1,0:T(8,128)(2,1)} collective-permute-done((bf16[64,1152]{1,0:T(8,128)(2,1)S(1)}, bf16[64,1152]{1,0:T(8,128)(2,1)}, u32[]{:S(2)}, u32[]{:S(2)}) %collective-permute-start.35) | collective-permute-done | bytes 147488 | tf_op jit(solution)/shard_map/ppermute | solution.py:29
  213.2 2.4 %shard_map.194.refs_0_ = f32[32,256]{1,0:T(8,128)S(1)} custom-call(s32[1,256]{1,0:T(1,128)S(1)} %reshape.134.slots, bf16[256,1024]{1,0:T(8,128)(2,1)S(1)} %reshape.135.x, bf16[64,1152]{1,0:T(8,128)(2,1)S(1)} %shard_map.193.refs_0_.refs_8_, bf16[64,1152]{1,0:T(8,128)(2,1)S(1)} %collective-permute-done.30.refs_1_.refs_9_, ...), custom_call_target="tpu_custom_call" | custom-call | tf_op jit(solution)/shard_map/pallas_call | solution.py:238
  217.4 7.2 %dot_general.5 = bf16[256,8192]{1,0:T(8,128)(2,1)} reshape(bf16[1,128,2,8192]{3,2,1,0:T(2,128)(2,1)} %param.25) | data formatting | bytes 8388608 | tf_op jit(solution)/shard_map/qsd,dk->qsk/dot_general | solution.py:380
  224.7 2.8 %collective-permute-start.40 = (f32[32,256]{1,0:T(8,128)S(1)}, f32[32,256]{1,0:T(8,128)S(1)}, u32[]{:S(2)}, u32[]{:S(2)}) collective-permute-start(f32[32,256]{1,0:T(8,128)S(1)} %shard_map.194.refs_0_), channel_id=1, source_target_pairs={{0,4},{1,5},{2,6},{3,7},{4,0},{5,1},{6,2},{7,3},{8,12},{9,13},{10,... | collective-permute-start | bytes 98312 | tf_op jit(solution)/shard_map/ppermute | solution.py:385
  229.7 3.5 %fusion.21.frozen = f32[256,128]{1,0:T(8,128)S(1)} fusion(bf16[256,8192]{1,0:T(8,128)(2,1)} %dot_general.5, bf16[8192,128]{1,0:T(8,128)(2,1)S(1)} %copy-done), kind=kOutput, calls=%fused_computation.78 | convolution fusion | flops 536870912 | bytes 6422528 | tf_op jit(solution)/shard_map/qsd,dk->qsk/dot_general | solution.py:380
  (132 shorter events, 74.1 us)
Async XLA Ops:
  3.2 51.7 %collective-permute-start.3 = (bf16[64,1152]{1,0:T(8,128)(2,1)}, bf16[64,1152]{1,0:T(8,128)(2,1)}, u32[]{:S(2)}, u32[]{:S(2)}) collective-permute-start(bf16[64,1152]{1,0:T(8,128)(2,1)} %pad_maximum_fusion.refs_0_), channel_id=1, source_target_pairs={{0,32},{32,64},{64,96},{96,128},{128,160},{160,192},{192,224},{224... | collective-permute-start | bytes 442376 | tf_op jit(solution)/shard_map/ppermute | solution.py:29
  13.5 83.7 %collective-permute-start.10 = (bf16[256,1152]{1,0:T(8,128)(2,1)}, bf16[256,1152]{1,0:T(8,128)(2,1)S(1)}, u32[]{:S(2)}, u32[]{:S(2)}) collective-permute-start(bf16[256,1152]{1,0:T(8,128)(2,1)} %get-tuple-element.27), channel_id=1, source_target_pairs={{0,8},{8,16},{16,24},{24,0},{1,9},{9,17},{17,25},{25,1},{2,10},{10... | collective-permute-start | bytes 1769480 | tf_op jit(solution)/shard_map/ppermute | solution.py:29
  14.0 83.2 %collective-permute-start.11 = (bf16[256,1152]{1,0:T(8,128)(2,1)}, bf16[256,1152]{1,0:T(8,128)(2,1)}, u32[]{:S(2)}, u32[]{:S(2)}) collective-permute-start(bf16[256,1152]{1,0:T(8,128)(2,1)} %get-tuple-element.28), channel_id=1, source_target_pairs={{0,16},{8,24},{16,0},{24,8},{1,17},{9,25},{17,1},{25,9},{2,18},{10... | collective-permute-start | bytes 1769480 | tf_op jit(solution)/shard_map/ppermute | solution.py:29
  16.4 80.8 %collective-permute-start.12 = (bf16[256,1152]{1,0:T(8,128)(2,1)}, bf16[256,1152]{1,0:T(8,128)(2,1)}, u32[]{:S(2)}, u32[]{:S(2)}) collective-permute-start(bf16[256,1152]{1,0:T(8,128)(2,1)} %get-tuple-element.29), channel_id=1, source_target_pairs={{0,24},{8,0},{16,8},{24,16},{1,25},{9,1},{17,9},{25,17},{2,26},{10... | collective-permute-start | bytes 1769480 | tf_op jit(solution)/shard_map/ppermute | solution.py:29
  16.4 26.5 %collective-permute-start.2 = (s32[2]{0:T(128)S(1)}, s32[2]{0:T(128)S(1)}, u32[]{:S(2)}, u32[]{:S(2)}) collective-permute-start(s32[2]{0:T(128)S(1)} %get-tuple-element.51), channel_id=1, source_target_pairs={{0,24},{8,0},{16,8},{24,16},{1,25},{9,1},{17,9},{25,17},{2,26},{10... | collective-permute-start | bytes 32 | tf_op jit(solution)/shard_map/ppermute | solution.py:29
  51.6 14.5 %collective-permute-start.4 = (bf16[64,1152]{1,0:T(8,128)(2,1)}, bf16[64,1152]{1,0:T(8,128)(2,1)S(1)}, u32[]{:S(2)}, u32[]{:S(2)}) collective-permute-start(bf16[64,1152]{1,0:T(8,128)(2,1)} %pad_maximum_fusion.refs_0_), channel_id=1, source_target_pairs={{0,64},{32,96},{64,128},{96,160},{128,192},{160,224},{192,0},{224,... | collective-permute-start | bytes 442376 | tf_op jit(solution)/shard_map/ppermute | solution.py:29
  54.9 20.8 %collective-permute-start.5 = (bf16[64,1152]{1,0:T(8,128)(2,1)}, bf16[64,1152]{1,0:T(8,128)(2,1)S(1)}, u32[]{:S(2)}, u32[]{:S(2)}) collective-permute-start(bf16[64,1152]{1,0:T(8,128)(2,1)} %pad_maximum_fusion.refs_0_), channel_id=1, source_target_pairs={{0,96},{32,128},{64,160},{96,192},{128,224},{160,0},{192,32},{224,... | collective-permute-start | bytes 442376 | tf_op jit(solution)/shard_map/ppermute | solution.py:29
  66.8 15.2 %collective-permute-start.6 = (bf16[64,1152]{1,0:T(8,128)(2,1)}, bf16[64,1152]{1,0:T(8,128)(2,1)S(1)}, u32[]{:S(2)}, u32[]{:S(2)}) collective-permute-start(bf16[64,1152]{1,0:T(8,128)(2,1)} %pad_maximum_fusion.refs_0_), channel_id=1, source_target_pairs={{0,128},{32,160},{64,192},{96,224},{128,0},{160,32},{192,64},{224,... | collective-permute-start | bytes 442376 | tf_op jit(solution)/shard_map/ppermute | solution.py:29
  76.4 14.6 %collective-permute-start.7 = (bf16[64,1152]{1,0:T(8,128)(2,1)}, bf16[64,1152]{1,0:T(8,128)(2,1)S(1)}, u32[]{:S(2)}, u32[]{:S(2)}) collective-permute-start(bf16[64,1152]{1,0:T(8,128)(2,1)} %pad_maximum_fusion.refs_0_), channel_id=1, source_target_pairs={{0,160},{32,192},{64,224},{96,0},{128,32},{160,64},{192,96},{224,1... | collective-permute-start | bytes 442376 | tf_op jit(solution)/shard_map/ppermute | solution.py:29
  82.6 10.1 %collective-permute-start.8 = (bf16[64,1152]{1,0:T(8,128)(2,1)}, bf16[64,1152]{1,0:T(8,128)(2,1)}, u32[]{:S(2)}, u32[]{:S(2)}) collective-permute-start(bf16[64,1152]{1,0:T(8,128)(2,1)} %pad_maximum_fusion.refs_0_), channel_id=1, source_target_pairs={{0,192},{32,224},{64,0},{96,32},{128,64},{160,96},{192,128},{224,1... | collective-permute-start | bytes 442376 | tf_op jit(solution)/shard_map/ppermute | solution.py:29
  105.3 11.3 %collective-permute-start.16 = (bf16[512,128]{1,0:T(8,128)(2,1)S(1)}, bf16[512,128]{1,0:T(8,128)(2,1)S(1)}, u32[]{:S(2)}, u32[]{:S(2)}) collective-permute-start(bf16[512,128]{1,0:T(8,128)(2,1)S(1)} %shard_map.190.refs_0_), channel_id=1, source_target_pairs={{0,4},{1,5},{2,6},{3,7},{4,0},{5,1},{6,2},{7,3},{8,12},{9,13},{10,... | collective-permute-start | bytes 393224 | tf_op jit(solution)/shard_map/ppermute | solution.py:335
  107.6 10.8 %collective-permute-start.17 = (bf16[512,128]{1,0:T(8,128)(2,1)S(1)}, bf16[512,128]{1,0:T(8,128)(2,1)S(1)}, u32[]{:S(2)}, u32[]{:S(2)}) collective-permute-start(bf16[512,128]{1,0:T(8,128)(2,1)S(1)} %shard_map.190.refs_0_), channel_id=1, source_target_pairs={{0,5},{1,4},{2,7},{3,6},{4,1},{5,0},{6,3},{7,2},{8,13},{9,12},{10,... | collective-permute-start | bytes 393224 | tf_op jit(solution)/shard_map/ppermute | solution.py:335
  108.5 11.9 %collective-permute-start.18 = (bf16[512,128]{1,0:T(8,128)(2,1)S(1)}, bf16[512,128]{1,0:T(8,128)(2,1)S(1)}, u32[]{:S(2)}, u32[]{:S(2)}) collective-permute-start(bf16[512,128]{1,0:T(8,128)(2,1)S(1)} %shard_map.190.refs_0_), channel_id=1, source_target_pairs={{0,6},{1,7},{2,4},{3,5},{4,2},{5,3},{6,0},{7,1},{8,14},{9,15},{10,... | collective-permute-start | bytes 393224 | tf_op jit(solution)/shard_map/ppermute | solution.py:335
  110.1 12.2 %collective-permute-start.19 = (bf16[512,128]{1,0:T(8,128)(2,1)S(1)}, bf16[512,128]{1,0:T(8,128)(2,1)S(1)}, u32[]{:S(2)}, u32[]{:S(2)}) collective-permute-start(bf16[512,128]{1,0:T(8,128)(2,1)S(1)} %shard_map.190.refs_0_), channel_id=1, source_target_pairs={{0,7},{1,6},{2,5},{3,4},{4,3},{5,2},{6,1},{7,0},{8,15},{9,14},{10,... | collective-permute-start | bytes 393224 | tf_op jit(solution)/shard_map/ppermute | solution.py:335
  125.7 10.4 %collective-permute-start.20 = (bf16[64,1152]{1,0:T(8,128)(2,1)S(1)}, bf16[64,1152]{1,0:T(8,128)(2,1)S(1)}, u32[]{:S(2)}, u32[]{:S(2)}) collective-permute-start(bf16[64,1152]{1,0:T(8,128)(2,1)S(1)} %get-tuple-element.31), channel_id=1, source_target_pairs={{0,32},{32,64},{64,96},{96,128},{128,160},{160,192},{192,224},{224... | collective-permute-start | bytes 442376 | tf_op jit(solution)/shard_map/ppermute | solution.py:29
  125.7 17.6 %collective-permute-start.21 = (bf16[64,1152]{1,0:T(8,128)(2,1)S(1)}, bf16[64,1152]{1,0:T(8,128)(2,1)S(1)}, u32[]{:S(2)}, u32[]{:S(2)}) collective-permute-start(bf16[64,1152]{1,0:T(8,128)(2,1)S(1)} %get-tuple-element.32), channel_id=1, source_target_pairs={{0,64},{32,96},{64,128},{96,160},{128,192},{160,224},{192,0},{224,... | collective-permute-start | bytes 442376 | tf_op jit(solution)/shard_map/ppermute | solution.py:29
  129.2 20.8 %collective-permute-start.22 = (bf16[64,1152]{1,0:T(8,128)(2,1)}, bf16[64,1152]{1,0:T(8,128)(2,1)S(1)}, u32[]{:S(2)}, u32[]{:S(2)}) collective-permute-start(bf16[64,1152]{1,0:T(8,128)(2,1)} %get-tuple-element.33), channel_id=1, source_target_pairs={{0,96},{32,128},{64,160},{96,192},{128,224},{160,0},{192,32},{224,... | collective-permute-start | bytes 442376 | tf_op jit(solution)/shard_map/ppermute | solution.py:29
  130.7 21.0 %collective-permute-start.23 = (bf16[64,1152]{1,0:T(8,128)(2,1)}, bf16[64,1152]{1,0:T(8,128)(2,1)S(1)}, u32[]{:S(2)}, u32[]{:S(2)}) collective-permute-start(bf16[64,1152]{1,0:T(8,128)(2,1)} %get-tuple-element.34), channel_id=1, source_target_pairs={{0,128},{32,160},{64,192},{96,224},{128,0},{160,32},{192,64},{224,... | collective-permute-start | bytes 442376 | tf_op jit(solution)/shard_map/ppermute | solution.py:29
  132.3 20.6 %collective-permute-start.24 = (bf16[64,1152]{1,0:T(8,128)(2,1)}, bf16[64,1152]{1,0:T(8,128)(2,1)S(1)}, u32[]{:S(2)}, u32[]{:S(2)}) collective-permute-start(bf16[64,1152]{1,0:T(8,128)(2,1)} %get-tuple-element.35), channel_id=1, source_target_pairs={{0,160},{32,192},{64,224},{96,0},{128,32},{160,64},{192,96},{224,1... | collective-permute-start | bytes 442376 | tf_op jit(solution)/shard_map/ppermute | solution.py:29
  136.2 23.1 %collective-permute-start.25 = (bf16[64,1152]{1,0:T(8,128)(2,1)}, bf16[64,1152]{1,0:T(8,128)(2,1)S(1)}, u32[]{:S(2)}, u32[]{:S(2)}) collective-permute-start(bf16[64,1152]{1,0:T(8,128)(2,1)} %get-tuple-element.36), channel_id=1, source_target_pairs={{0,192},{32,224},{64,0},{96,32},{128,64},{160,96},{192,128},{224,1... | collective-permute-start | bytes 442376 | tf_op jit(solution)/shard_map/ppermute | solution.py:29
  143.3 17.9 %collective-permute-start.26 = (bf16[64,1152]{1,0:T(8,128)(2,1)}, bf16[64,1152]{1,0:T(8,128)(2,1)S(1)}, u32[]{:S(2)}, u32[]{:S(2)}) collective-permute-start(bf16[64,1152]{1,0:T(8,128)(2,1)} %get-tuple-element.37), channel_id=1, source_target_pairs={{0,224},{32,0},{64,32},{96,64},{128,96},{160,128},{192,160},{224,1... | collective-permute-start | bytes 442376 | tf_op jit(solution)/shard_map/ppermute | solution.py:29
  178.2 12.8 %collective-permute-start.30 = (bf16[64,1152]{1,0:T(8,128)(2,1)S(1)}, bf16[64,1152]{1,0:T(8,128)(2,1)S(1)}, u32[]{:S(2)}, u32[]{:S(2)}) collective-permute-start(bf16[64,1152]{1,0:T(8,128)(2,1)S(1)} %shard_map.193.refs_0_.refs_8_), channel_id=1, source_target_pairs={{0,32},{32,64},{64,96},{96,128},{128,160},{160,192},{192,224},{224... | collective-permute-start | bytes 442376 | tf_op jit(solution)/shard_map/ppermute | solution.py:29
  180.9 18.2 %collective-permute-start.31 = (bf16[64,1152]{1,0:T(8,128)(2,1)S(1)}, bf16[64,1152]{1,0:T(8,128)(2,1)S(1)}, u32[]{:S(2)}, u32[]{:S(2)}) collective-permute-start(bf16[64,1152]{1,0:T(8,128)(2,1)S(1)} %shard_map.193.refs_0_.refs_8_), channel_id=1, source_target_pairs={{0,64},{32,96},{64,128},{96,160},{128,192},{160,224},{192,0},{224,... | collective-permute-start | bytes 442376 | tf_op jit(solution)/shard_map/ppermute | solution.py:29
  181.7 21.9 %collective-permute-start.32 = (bf16[64,1152]{1,0:T(8,128)(2,1)S(1)}, bf16[64,1152]{1,0:T(8,128)(2,1)S(1)}, u32[]{:S(2)}, u32[]{:S(2)}) collective-permute-start(bf16[64,1152]{1,0:T(8,128)(2,1)S(1)} %shard_map.193.refs_0_.refs_8_), channel_id=1, source_target_pairs={{0,96},{32,128},{64,160},{96,192},{128,224},{160,0},{192,32},{224,... | collective-permute-start | bytes 442376 | tf_op jit(solution)/shard_map/ppermute | solution.py:29
  183.0 24.2 %collective-permute-start.33 = (bf16[64,1152]{1,0:T(8,128)(2,1)S(1)}, bf16[64,1152]{1,0:T(8,128)(2,1)S(1)}, u32[]{:S(2)}, u32[]{:S(2)}) collective-permute-start(bf16[64,1152]{1,0:T(8,128)(2,1)S(1)} %shard_map.193.refs_0_.refs_8_), channel_id=1, source_target_pairs={{0,128},{32,160},{64,192},{96,224},{128,0},{160,32},{192,64},{224,... | collective-permute-start | bytes 442376 | tf_op jit(solution)/shard_map/ppermute | solution.py:29
  187.6 19.6 %collective-permute-start.34 = (bf16[64,1152]{1,0:T(8,128)(2,1)S(1)}, bf16[64,1152]{1,0:T(8,128)(2,1)S(1)}, u32[]{:S(2)}, u32[]{:S(2)}) collective-permute-start(bf16[64,1152]{1,0:T(8,128)(2,1)S(1)} %shard_map.193.refs_0_.refs_8_), channel_id=1, source_target_pairs={{0,160},{32,192},{64,224},{96,0},{128,32},{160,64},{192,96},{224,1... | collective-permute-start | bytes 442376 | tf_op jit(solution)/shard_map/ppermute | solution.py:29
  191.0 21.0 %collective-permute-start.35 = (bf16[64,1152]{1,0:T(8,128)(2,1)S(1)}, bf16[64,1152]{1,0:T(8,128)(2,1)}, u32[]{:S(2)}, u32[]{:S(2)}) collective-permute-start(bf16[64,1152]{1,0:T(8,128)(2,1)S(1)} %shard_map.193.refs_0_.refs_8_), channel_id=1, source_target_pairs={{0,192},{32,224},{64,0},{96,32},{128,64},{160,96},{192,128},{224,1... | collective-permute-start | bytes 442376 | tf_op jit(solution)/shard_map/ppermute | solution.py:29
  199.2 14.0 %collective-permute-start.36 = (bf16[64,1152]{1,0:T(8,128)(2,1)S(1)}, bf16[64,1152]{1,0:T(8,128)(2,1)}, u32[]{:S(2)}, u32[]{:S(2)}) collective-permute-start(bf16[64,1152]{1,0:T(8,128)(2,1)S(1)} %shard_map.193.refs_0_.refs_8_), channel_id=1, source_target_pairs={{0,224},{32,0},{64,32},{96,64},{128,96},{160,128},{192,160},{224,1... | collective-permute-start | bytes 442376 | tf_op jit(solution)/shard_map/ppermute | solution.py:29
  215.5 12.4 %collective-permute-start.37 = (f32[32,256]{1,0:T(8,128)S(1)}, f32[32,256]{1,0:T(8,128)S(1)}, u32[]{:S(2)}, u32[]{:S(2)}) collective-permute-start(f32[32,256]{1,0:T(8,128)S(1)} %shard_map.194.refs_0_), channel_id=1, source_target_pairs={{0,1},{1,0},{2,3},{3,2},{4,5},{5,4},{6,7},{7,6},{8,9},{9,8},{10,11... | collective-permute-start | bytes 98312 | tf_op jit(solution)/shard_map/ppermute | solution.py:385
  215.6 13.9 %collective-permute-start.38 = (f32[32,256]{1,0:T(8,128)S(1)}, f32[32,256]{1,0:T(8,128)S(1)}, u32[]{:S(2)}, u32[]{:S(2)}) collective-permute-start(f32[32,256]{1,0:T(8,128)S(1)} %shard_map.194.refs_0_), channel_id=1, source_target_pairs={{0,2},{1,3},{2,0},{3,1},{4,6},{5,7},{6,4},{7,5},{8,10},{9,11},{10,... | collective-permute-start | bytes 98312 | tf_op jit(solution)/shard_map/ppermute | solution.py:385
  224.6 8.6 %collective-permute-start.39 = (f32[32,256]{1,0:T(8,128)S(1)}, f32[32,256]{1,0:T(8,128)S(1)}, u32[]{:S(2)}, u32[]{:S(2)}) collective-permute-start(f32[32,256]{1,0:T(8,128)S(1)} %shard_map.194.refs_0_), channel_id=1, source_target_pairs={{0,3},{1,2},{2,1},{3,0},{4,7},{5,6},{6,5},{7,4},{8,11},{9,10},{10,... | collective-permute-start | bytes 98312 | tf_op jit(solution)/shard_map/ppermute | solution.py:385
  224.7 8.5 %collective-permute-start.40 = (f32[32,256]{1,0:T(8,128)S(1)}, f32[32,256]{1,0:T(8,128)S(1)}, u32[]{:S(2)}, u32[]{:S(2)}) collective-permute-start(f32[32,256]{1,0:T(8,128)S(1)} %shard_map.194.refs_0_), channel_id=1, source_target_pairs={{0,4},{1,5},{2,6},{3,7},{4,0},{5,1},{6,2},{7,3},{8,12},{9,13},{10,... | collective-permute-start | bytes 98312 | tf_op jit(solution)/shard_map/ppermute | solution.py:385
  (33 other events, 585.6 us)
